TPU v7x, 256 devices: a whole 4x4x8 slice. The times are simulated.
256 devices in a mesh: tgt: 8 (over y, x_hi), sup: 32 (over z, x_lo, core).
Axes of the slice: x: 4 (x_hi: 2, x_lo: 2; x = x_hi * 2 + x_lo), y: 4, z: 8, core: 2. Of those that a mesh axis runs over, the one named last changes fastest.
Arguments:
- support: float32 [256, 3, 1024], P(('sup', 'tgt')), may hold values from -14 to 14
- coeffs: float32 [256, 100], P('sup'), may hold values from -1.25 to 1.25
- targets: float32 [256, 3, 1024], P(('tgt', 'sup')), may hold values from -14 to 14
- labels: float32 [256, 100], P(('tgt', 'sup')), may hold values from -5 to 5
Outputs:
- support_grad: float32 [256, 3, 1024], P(('sup', 'tgt'))
- residual: float32 [256, 100], P(('tgt', 'sup'))
All inputs are finite; a program needn't handle non-finite values.
Results may differ from a plain program's by a relative error of at most 0.000064.
Values sent between devices are 32-bit elements; how exact they have to be, the bound alone decides.
A program may use at most 128 MiB of HBM per device.

v0:
```python
import math

import jax
import jax.numpy as jnp
from jax import lax
from jax.sharding import PartitionSpec as P

SIDE = 32
DEPTH = 3


WEIGHT_VAR = 1.6
BIAS_VAR = 0.1


def spread(values):
    side_cells = values.shape[0]
    padded = jnp.pad(values, ((1, 1), (1, 1), (0, 0)))
    summed = jnp.zeros_like(values)
    for row_shift in range(3):
        for col_shift in range(3):
            summed = (
                summed
                + padded[row_shift : row_shift + side_cells, col_shift : col_shift + side_cells]
            )
    return summed / 9.0


def self_levels(images):
    image_count = images.shape[0]
    energy = jnp.mean(images * images, axis=1)
    kernel_level = WEIGHT_VAR * spread(energy.T.reshape(SIDE, SIDE, image_count)) + BIAS_VAR
    levels = [kernel_level]
    for layer_idx in range(DEPTH - 1):
        activated = 2.0 / math.pi * jnp.arcsin(2.0 * kernel_level / (1.0 + 2.0 * kernel_level))
        kernel_level = WEIGHT_VAR * spread(activated) + BIAS_VAR
        levels.append(kernel_level)
    return levels


def pair_kernel(support, targets):
    sup_count = support.shape[0]
    tgt_count = targets.shape[0]
    sup_levels = self_levels(support)
    tgt_levels = self_levels(targets)
    products = (
        jnp.einsum("scp,tcp->pst", support, targets, precision=lax.Precision.HIGHEST)
        / support.shape[1]
    )
    kernel_level = (
        WEIGHT_VAR * spread(products.reshape(SIDE, SIDE, sup_count * tgt_count)) + BIAS_VAR
    )
    activated = kernel_level
    for layer_idx in range(DEPTH):
        sup_gain = lax.rsqrt(1.0 + 2.0 * sup_levels[layer_idx])
        tgt_gain = lax.rsqrt(1.0 + 2.0 * tgt_levels[layer_idx])
        correlation = (
            2.0
            * kernel_level.reshape(SIDE, SIDE, sup_count, tgt_count)
            * sup_gain[:, :, :, None]
            * tgt_gain[:, :, None, :]
        )
        activated = 2.0 / math.pi * jnp.arcsin(correlation)
        if layer_idx + 1 < DEPTH:
            kernel_level = (
                WEIGHT_VAR * spread(activated.reshape(SIDE, SIDE, sup_count * tgt_count)) + BIAS_VAR
            )
    return WEIGHT_VAR * jnp.mean(activated, axis=(0, 1)) + BIAS_VAR


def product(left, right):
    return jnp.dot(left, right, precision=lax.Precision.HIGHEST, preferred_element_type=jnp.float32)


def local(support, coeffs, targets, labels):
    tgt_dev = targets.shape[0]
    block = lax.all_gather(support, "tgt", axis=0, tiled=True)
    group, group_labels = (
        lax.all_gather(targets, "sup", axis=0, tiled=True),
        lax.all_gather(labels, "sup", axis=0, tiled=True),
    )
    theta, pullback = jax.vjp(lambda images: pair_kernel(images, group), block)
    predicted = lax.psum(product(theta.T, coeffs), "sup")
    misfit = predicted - group_labels
    residual = lax.dynamic_slice_in_dim(misfit, lax.axis_index("sup") * tgt_dev, tgt_dev, 0)
    block_grad = pullback(product(coeffs, misfit.T))[0]
    support_grad = lax.psum_scatter(block_grad, "tgt", scatter_dimension=0, tiled=True)
    return (support_grad, residual)


def solution(mesh):
    return jax.shard_map(
        local,
        mesh=mesh,
        in_specs=(
            P(("sup", "tgt"), None, None),
            P("sup", None),
            P(("tgt", "sup"), None, None),
            P(("tgt", "sup"), None),
        ),
        out_specs=(P(("sup", "tgt"), None, None), P(("tgt", "sup"), None)),
        check_vma=False,
    )
```

profile of v0, /device:TPU:2, one launch (start us, length us, event | category | flops | bytes accessed | tf_op | source)
XLA Modules:
  0.0 546.5 jit_solution(2418600961972552821)
XLA Ops:
  7.9 35.5 %all_gather.10 = f32[32,3,1024]{2,1,0:T(4,128)S(1)} all-gather(f32[1,3,1024]{2,1,0:T(4,128)S(1)} %copy.59), channel_id=1, replica_groups=mesh['tgt'=8,'sup'=32] {'sup'}, dimensions={0}, use_global_device_ids=true | all-gather | bytes 405504 | tf_op jit(solution)/shard_map/all_gather | solution.py:79
  43.8 13.8 %copy.61 = f32[32,3,1024]{1,0,2:T(8,128)} copy(f32[32,3,1024]{2,1,0:T(4,128)S(1)} %all_gather.10) | data formatting | bytes 786432 | tf_op jit(solution)/shard_map/all_gather | solution.py:79
  57.6 34.7 %all_gather.9 = f32[8,3,1024]{2,1,0:T(4,128)S(1)} all-gather(f32[1,3,1024]{2,1,0:T(4,128)S(1)} %copy.58), channel_id=1, replica_groups=mesh['tgt'=8,'sup'=32] {'tgt'}, dimensions={0}, use_global_device_ids=true | all-gather | bytes 110592 | tf_op jit(solution)/shard_map/all_gather | solution.py:77
  106.9 4.0 broadcast_multiply_fusion.2
  113.6 4.2 mul.393
  117.8 30.2 %convolution_multiply_fusion = f32[1024,8,32]{2,1,0:T(8,128)} fusion(f32[8,3,1024]{1,0,2:T(8,128)} %copy.60, f32[32,3,1024]{1,0,2:T(8,128)} %copy.61), kind=kOutput, calls=%fused_computation.3 | convolution fusion | flops 9699328 | bytes 1540096 | tf_op jit(solution)/shard_map/jvp(scp,tcp->pst)/dot_general | solution.py:47
  147.9 4.2 reshape.78
  156.6 4.2 mul.415
  165.6 4.2 mul.409
  189.5 9.1 %add_multiply_fusion.3 = (f32[32,32,256]{2,1,0:T(8,128)S(1)}, f32[32,32,256]{2,1,0:T(8,128)}) fusion(f32[32,32,256]{2,1,0:T(8,128)S(1)} %mul.400, f32[32,32,256]{2,1,0:T(8,128)} %mul.393, f32[32,32,256]{2,1,0:T(8,128)} %reshape.78), kind=kLoop, calls=%fused_computation.93 | loop fusion | flops 4718592 | bytes 5242880 | tf_op jit(solution)/shard_map/jvp()/mul | solution.py:63
  204.9 103.8 %psum.7 = f32[32,100]{1,0:T(8,128)S(1)} all-reduce(f32[32,100]{1,0:T(8,128)S(1)} %fusion.136), channel_id=1, replica_groups=mesh['tgt'=8,'sup'=32] {'sup'}, use_global_device_ids=true, to_apply=%region_3.4 | all-reduce | flops 3200 | bytes 25600 | tf_op jit(solution)/shard_map/psum | solution.py:83
  308.7 34.5 %all-gather = f32[32,1,100]{2,1,0:T(1,128)S(1)} all-gather(f32[1,1,100]{2,1,0:T(1,128)S(1)} %bitcast.46), channel_id=1, replica_groups=mesh['tgt'=8,'sup'=32] {'sup'}, dimensions={0}, use_global_device_ids=true | all-gather | bytes 13200 | tf_op jit(solution)/shard_map/all_gather | solution.py:80
  345.9 5.0 multiply_reduce_fusion
  354.5 4.2 mul.441
  364.5 4.3 mul.447
  371.3 6.8 %multiply_multiply_fusion.1 = (f32[32,32,256]{2,1,0:T(8,128)}, f32[32,32,256]{2,1,0:T(8,128)}) fusion(f32[32,32,256]{2,1,0:T(8,128)} %mul.447, f32[32,32,256]{2,1,0:T(8,128)S(1)} %copy-done.7, f32[32,32,256]{2,1,0:T(8,128)S(1)} %copy-done.10, f32[32,32,256]{2,1,0:T(8,128)S(1)} %copy-done.9, f32[32,32,256]{2,1,0:T(8,128)} %copy-done.12, ...), kind=kLoop, calls=%fused_computation.85 | loop fusion | flops 4194304 | bytes 8388608 | tf_op jit(solution)/shard_map/transpose(jvp())/div | solution.py:26
  378.1 3.9 mul.465
  382.2 5.7 %multiply_reduce_fusion.1 = f32[32,32,8]{2,1,0:T(8,128)S(1)} fusion(f32[32,32,8,32]{3,2,1,0:T(8,128)} %mul.465, f32[32,32,8,32]{3,2,1,0:T(8,128)} %reshape.82, f32[32,32,32]{2,1,0:T(8,128)S(1)} %copy-done.28, f32[32,32,8]{2,1,0:T(8,128)S(1)} %copy-done.21), kind=kLoop, calls=%fused_computation.1 | loop fusion | flops 2613248 | bytes 2293760 | tf_op jit(solution)/shard_map/transpose(jvp())/reduce_sum | solution.py:58
  393.6 4.3 mul.453
  400.4 7.0 %multiply_multiply_fusion = (f32[32,32,256]{2,1,0:T(8,128)}, f32[32,32,256]{2,1,0:T(8,128)}) fusion(f32[32,32,256]{2,1,0:T(8,128)} %mul.453, f32[32,32,256]{2,1,0:T(8,128)S(1)} %copy-done.3, f32[32,32,256]{2,1,0:T(8,128)S(1)} %copy-done.5, f32[32,32,256]{2,1,0:T(8,128)S(1)} %copy-done.4, f32[32,32,256]{2,1,0:T(8,128)} %get-tuple-element.16, ...), kind=kLoop, calls=%fused_computation.84 | loop fusion | flops 4194304 | bytes 8388608 | tf_op jit(solution)/shard_map/transpose(jvp())/div | solution.py:26
  407.4 4.1 mul.456
  411.5 5.8 %multiply_reduce_fusion.2 = f32[32,32,8]{2,1,0:T(8,128)S(1)} fusion(f32[32,32,8,32]{3,2,1,0:T(8,128)} %mul.456, f32[32,32,8,32]{3,2,1,0:T(8,128)} %reshape.81, f32[32,32,32]{2,1,0:T(8,128)S(1)} %copy-done.26, f32[32,32,8]{2,1,0:T(8,128)S(1)} %copy-done.17), kind=kLoop, calls=%fused_computation.2 | loop fusion | flops 2613248 | bytes 2293760 | tf_op jit(solution)/shard_map/transpose(jvp())/reduce_sum | solution.py:58
  421.8 29.1 %fusion.137 = f32[1024,8,3]{1,2,0:T(4,128)S(1)} fusion(f32[1024,8,32]{2,1,0:T(8,128)} %div.109, f32[32,3,1024]{1,0,2:T(8,128)} %copy.61), kind=kOutput, calls=%fused_computation.291 | convolution fusion | flops 9437184 | bytes 1540096 | tf_op jit(solution)/shard_map/transpose(jvp(scp,tcp->pst))/dot_general | solution.py:47
  453.5 84.0 %all-reduce.66.cloned.1.call-done = f32[8,3,1024]{2,1,0:T(4,128)} async-done(((f32[8,3,1024]{2,1,0:T(4,128)}), f32[8,3,1024]{2,1,0:T(4,128)}) %all-reduce.66.cloned.1.call-update) | async-done | bytes 98320
  (142 shorter events, 85.3 us)
Async XLA Ops:
  7.2 197.5 %copy-start = (f32[8,100]{1,0:T(8,128)S(1)}, f32[8,100]{1,0:T(8,128)}, u32[]{:S(2)}) copy-start(f32[8,100]{1,0:T(8,128)} %param.5) | copy-start | bytes 9604
  7.2 530.3 %all-reduce.66.cloned.1.call-start = ((), (), s32[]{:S(2)}) async-start(), calls=%async_computation | async-start | bytes 262144
  43.8 13.8 %copy-start.35 = (f32[1,3,1024]{2,0,1:T(1,128)S(1)}, f32[1,3,1024]{2,0,1:T(1,128)}, u32[]{:S(2)}) copy-start(f32[1,3,1024]{2,0,1:T(1,128)} %param.4) | copy-start | bytes 36868
  105.6 83.8 %copy-start.2 = (f32[32,32,256]{2,1,0:T(8,128)}, f32[32,32,256]{2,1,0:T(8,128)S(1)}, u32[]{:S(2)}) copy-start(f32[32,32,256]{2,1,0:T(8,128)S(1)} %mul.400) | copy-start | bytes 3145732
  110.9 6.9 %copy-start.16 = (f32[32,32,8]{2,1,0:T(8,128)}, f32[32,32,8]{2,1,0:T(8,128)S(1)}, u32[]{:S(2)}) copy-start(f32[32,32,8]{2,1,0:T(8,128)S(1)} %get-tuple-element.28) | copy-start | bytes 98308
  110.9 49.9 %copy-start.14 = (f32[32,32,8]{2,1,0:T(8,128)}, f32[32,32,8]{2,1,0:T(8,128)S(1)}, u32[]{:S(2)}) copy-start(f32[32,32,8]{2,1,0:T(8,128)S(1)} %get-tuple-element.29) | copy-start | bytes 98308
  154.3 6.4 %copy-start.27 = (f32[32,32,32]{2,1,0:T(8,128)}, f32[32,32,32]{2,1,0:T(8,128)S(1)}, u32[]{:S(2)}) copy-start(f32[32,32,32]{2,1,0:T(8,128)S(1)} %copy.65) | copy-start | bytes 393220
  163.0 6.8 %copy-start.20 = (f32[32,32,8]{2,1,0:T(8,128)}, f32[32,32,8]{2,1,0:T(8,128)S(1)}, u32[]{:S(2)}) copy-start(f32[32,32,8]{2,1,0:T(8,128)S(1)} %get-tuple-element.24) | copy-start | bytes 98308
  163.0 6.8 %copy-start.18 = (f32[32,32,8]{2,1,0:T(8,128)}, f32[32,32,8]{2,1,0:T(8,128)S(1)}, u32[]{:S(2)}) copy-start(f32[32,32,8]{2,1,0:T(8,128)S(1)} %get-tuple-element.25) | copy-start | bytes 98308
  189.4 9.1 %copy-start.6 = (f32[32,32,256]{2,1,0:T(8,128)S(1)}, f32[32,32,256]{2,1,0:T(8,128)}, u32[]{:S(2)}) copy-start(f32[32,32,256]{2,1,0:T(8,128)} %mul.415) | copy-start | bytes 3145732
  189.5 9.1 %copy-start.8 = (f32[32,32,256]{2,1,0:T(8,128)S(1)}, f32[32,32,256]{2,1,0:T(8,128)}, u32[]{:S(2)}) copy-start(f32[32,32,256]{2,1,0:T(8,128)} %mul.409) | copy-start | bytes 3145732
  198.5 110.2 %copy-start.36 = (f32[1,100]{1,0:T(1,128)S(1)}, f32[1,100]{1,0:T(1,128)}, u32[]{:S(2)}) copy-start(f32[1,100]{1,0:T(1,128)} %param.7) | copy-start | bytes 1204
  361.9 6.9 %copy-start.10 = (f32[32,32,256]{2,1,0:T(8,128)S(1)}, f32[32,32,256]{2,1,0:T(8,128)}, u32[]{:S(2)}) copy-start(f32[32,32,256]{2,1,0:T(8,128)} %get-tuple-element.23) | copy-start | bytes 3145732
  364.5 6.8 %copy-start.7 = (f32[32,32,256]{2,1,0:T(8,128)S(1)}, f32[32,32,256]{2,1,0:T(8,128)}, u32[]{:S(2)}) copy-start(f32[32,32,256]{2,1,0:T(8,128)} %mul.415) | copy-start | bytes 3145732
  364.5 6.8 %copy-start.9 = (f32[32,32,256]{2,1,0:T(8,128)S(1)}, f32[32,32,256]{2,1,0:T(8,128)}, u32[]{:S(2)}) copy-start(f32[32,32,256]{2,1,0:T(8,128)} %mul.409) | copy-start | bytes 3145732
  382.2 5.8 %copy-start.19 = (f32[32,32,8]{2,1,0:T(8,128)S(1)}, f32[32,32,8]{2,1,0:T(8,128)}, u32[]{:S(2)}) copy-start(f32[32,32,8]{2,1,0:T(8,128)} %copy-done.18) | copy-start | bytes 98308
  391.1 6.9 %copy-start.5 = (f32[32,32,256]{2,1,0:T(8,128)S(1)}, f32[32,32,256]{2,1,0:T(8,128)}, u32[]{:S(2)}) copy-start(f32[32,32,256]{2,1,0:T(8,128)} %get-tuple-element.27) | copy-start | bytes 3145732
  393.6 6.8 %copy-start.3 = (f32[32,32,256]{2,1,0:T(8,128)S(1)}, f32[32,32,256]{2,1,0:T(8,128)}, u32[]{:S(2)}) copy-start(f32[32,32,256]{2,1,0:T(8,128)} %copy-done.2) | copy-start | bytes 3145732
  393.6 6.8 %copy-start.4 = (f32[32,32,256]{2,1,0:T(8,128)S(1)}, f32[32,32,256]{2,1,0:T(8,128)}, u32[]{:S(2)}) copy-start(f32[32,32,256]{2,1,0:T(8,128)} %mul.393) | copy-start | bytes 3145732
  411.5 5.8 %copy-start.15 = (f32[32,32,8]{2,1,0:T(8,128)S(1)}, f32[32,32,8]{2,1,0:T(8,128)}, u32[]{:S(2)}) copy-start(f32[32,32,8]{2,1,0:T(8,128)} %copy-done.14) | copy-start | bytes 98308
  411.5 5.8 %copy-start.24 = (f32[32,32,8]{2,1,0:T(8,128)S(1)}, f32[32,32,8]{2,1,0:T(8,128)}, u32[]{:S(2)}) copy-start(f32[32,32,8]{2,1,0:T(8,128)} %copy-done.23) | copy-start | bytes 98308
  411.5 5.8 %copy-start.31 = (f32[34,34,8]{2,1,0:T(8,128)S(1)}, f32[34,34,8]{2,1,0:T(8,128)}, u32[]{:S(2)}) copy-start(f32[34,34,8]{2,1,0:T(8,128)} %pad_add_fusion.22) | copy-start | bytes 110980
  421.8 30.6 %copy-start.37 = (u32[256]{0:T(256)S(1)}, u32[256]{0:T(256)}, u32[]{:S(2)}) copy-start(u32[256]{0:T(256)} %constant.232) | copy-start | bytes 3076
  421.8 117.7 %copy-start.1 = (f32[8,100]{1,0:T(8,128)S(1)}, f32[8,100]{1,0:T(8,128)}, u32[]{:S(2)}) copy-start(f32[8,100]{1,0:T(8,128)} %param.5) | copy-start | bytes 9604
  (15 other events, 45.8 us)
Sparse Core Ops, SparseCore 0:
  452.5 84.9 all-reduce.65
where the time goes:
time: 556 us; the launch traced here: 546 us
  blocking collectives  208 us (37%)
  local copies, waits for them, and re-layouts  108 us (19%)
  waiting for transfers between devices  84 us (15%)
  other arithmetic  71.5 us (13%)
  matrix products  59.7 us (11%)
  between operations  14.7 us (3%)
    psum x1, blocking collectives, local(): predicted = lax.psum(product(theta.T, coeffs), 'sup')  104 us
    unnamed x2, waiting for transfers between devices  84 us
    dot_general x2, matrix products, pair_kernel(): jnp.einsum('scp,tcp->pst', support, targets, precision=lax.Precision.HIGH...  59.3 us
    mul x18, local copies, waits for them, and re-layouts, pair_kernel(): 2.0 * kernel_level.reshape(SIDE, SIDE, sup_count, tgt_count)  58.1 us
    all_gather x1, blocking collectives, local(): lax.all_gather(targets, 'sup', axis=0, tiled=True)  35.5 us
    all_gather x1, blocking collectives, local(): block = lax.all_gather(support, 'tgt', axis=0, tiled=True)  34.7 us
    all_gather x1, blocking collectives, local(): lax.all_gather(labels, 'sup', axis=0, tiled=True)  34.5 us
    div x6, other arithmetic, spread(): return summed / 9.0  17.9 us
  transfers between devices with their start and end apart: 1, of which 1 were waited for; matrix products, arithmetic and copies ran while one was open for 0% of the time, Pallas kernels for 0%

commit v1 on v0

v1 whole, which is shorter than its diff:
```python
import math

import jax
import jax.numpy as jnp
from jax import lax
from jax.experimental import pallas as pl
from jax.experimental.pallas import tpu as pltpu
from jax.sharding import PartitionSpec as P

f32 = jnp.float32
bf16 = jnp.bfloat16
MESH = pl.DeviceIdType.MESH
HIGHEST = lax.Precision.HIGHEST

WEIGHT_VAR = 1.6
BIAS_VAR = 0.1
LABELS = 100

GROUP = 16
ROWS = 24
SPREAD = WEIGHT_VAR / 9.0
PROD = SPREAD / 3.0
ALPHA = SPREAD * 2.0 / math.pi
BETA = WEIGHT_VAR / 1024.0 * 2.0 / math.pi

WIDE = (
    1.5707962162062898, -0.9999815161013006, 0.7848809620778067, -0.6609690948852064, 0.5565553788659177,
    -0.42358122423204403, 0.252084788157994, -0.0972640965051769, 0.017478656801048167,
)
NARROW = (
    1.5660394665702648, -0.9597383006319578, 0.6362998416714283, -0.3442600430796345, 0.12171201192018792,
    -0.020052988434709065,
)


def horner(w, coefs, scale):
    total = jnp.full_like(w, coefs[-1] * scale)
    for coef in coefs[-2::-1]:
        total = total * w + coef * scale
    return total


def lanes(shape):
    return lax.broadcasted_iota(jnp.int32, shape, len(shape) - 1)


def roll_lanes(x, shift):
    flat = x.reshape(-1, 128)
    return pltpu.roll(flat, shift, 1).reshape(x.shape)


def col_sum(x, masks):
    return x + roll_lanes(x, 1) * masks[0] + roll_lanes(x, 127) * masks[1]


def col_masks():
    col = lanes((1, 128)) % 32
    return (col != 0).astype(f32), (col != 31).astype(f32)


def self_chain(energy, box):
    gains, slopes = [], []
    level = box(energy) + BIAS_VAR
    for layer in range(3):
        gain = lax.rsqrt(1.0 + 2.0 * level)
        gains.append(gain)
        if layer < 2:
            square = gain * gain
            root = lax.rsqrt(1.0 + 4.0 * level)
            w = (1.0 + 4.0 * level) * root * square
            value = 2.0 * level * square * horner(w, NARROW if layer else WIDE, ALPHA)
            slopes.append((4.0 / math.pi * SPREAD) * square * root)
            level = box(value) + BIAS_VAR
    return gains, slopes


def box_natural(x, masks):
    h = col_sum(x, masks)
    lane = lanes((1, 1, 1, 128))
    zero = jnp.zeros_like(h[:, :1])
    above = roll_lanes(h, 32)
    below = roll_lanes(h, 96)
    above = jnp.where(lane < 32, jnp.concatenate([zero, above[:, :-1]], 1), above)
    below = jnp.where(lane >= 96, jnp.concatenate([below[:, 1:], zero], 1), below)
    return h + above + below


def prepare_supports(sbuf, srep, gsrep, slope_ref, masks):
    for sg in range(2):
        chans = [
            jnp.stack([sbuf[pl.ds(sg * 8 * ROWS + c * 8 + g, 8, stride=ROWS), :] for g in range(8)])[None]
            for c in range(3)
        ]
        energy = (chans[0] * chans[0] + chans[1] * chans[1] + chans[2] * chans[2]) * PROD
        gains, slopes = self_chain(energy, lambda x: box_natural(x, masks))
        for layer in range(2):
            slope_ref[layer, sg] = slopes[layer][0]
        for layer in range(3):
            slope_ref[2 + layer, sg] = -(gains[layer] * gains[layer])[0]
        lane = lanes((1, 128))
        low, even = lane < 64, (lane // 32) % 2 == 0
        for q in range(6):
            src = chans[q][0] * PROD if q < 3 else gains[q - 3][0] * 2.0
            dst = srep if q < 3 else gsrep
            turned = roll_lanes(src, 64)
            first, second = jnp.where(low, src, turned), jnp.where(low, turned, src)
            t1, t2 = roll_lanes(first, 32), roll_lanes(second, 32)
            reps = (jnp.where(even, first, t1), jnp.where(even, t1, first), jnp.where(even, second, t2), jnp.where(even, t2, second))
            for j in range(4):
                for g in range(8):
                    dst[sg, q % 3, g * 4 + j] = reps[j][g]


def prepare_targets(tbuf, tq, gt, masks):
    lane = lanes((1, 128))
    low, even = lane < 64, (lane // 32) % 2 == 0
    for tg in range(4):
        a = [tbuf[4 * tg + i] for i in range(4)]
        p = [None] * 4
        for i in range(2):
            p[i] = jnp.where(low, a[i], pltpu.roll(a[i + 2], 64, 1))
            p[i + 2] = jnp.where(low, pltpu.roll(a[i], 64, 1), a[i + 2])
        for k in range(2):
            b0 = jnp.where(even, p[2 * k], pltpu.roll(p[2 * k + 1], 32, 1))
            b1 = jnp.where(even, pltpu.roll(p[2 * k], 96, 1), p[2 * k + 1])
            for c in range(3):
                tq[2 * k, c, tg] = b0[c * 8 : c * 8 + 8]
                tq[2 * k + 1, c, tg] = b1[c * 8 : c * 8 + 8]
    x = [[tq[j, c].reshape(32, 128) for j in range(4)] for c in range(3)]
    energy = [(x[0][j] * x[0][j] + x[1][j] * x[1][j] + x[2][j] * x[2][j]) * PROD for j in range(4)]
    g = lax.broadcasted_iota(jnp.int32, (32, 128), 0) % 8
    not_first, not_last = (g != 0).astype(f32), (g != 7).astype(f32)

    def box(values):
        h = [col_sum(values[j * 32 : j * 32 + 32], masks) for j in range(4)]
        above = [pltpu.roll(h[3], 1, 0) * not_first] + h[:3]
        below = h[1:] + [pltpu.roll(h[0], 31, 0) * not_last]
        return jnp.concatenate([h[j] + above[j] + below[j] for j in range(4)], 0)

    gains, _ = self_chain(jnp.concatenate(energy, 0), box)
    for layer in range(3):
        for j in range(4):
            gt[j, layer] = gains[layer][j * 32 : j * 32 + 32].reshape(4, 8, 128)


def target_rows(ref, q, tg, first, count):
    return jnp.concatenate([ref[r % 4, q, tg, pl.ds(r // 4, 1), :][None] for r in range(first, first + count)], 0)


CHUNK = 8


def forward_unit(u, sg, tg, srep, gsrep, tq, gt, xs, rs, hbuf, thacc, masks):
    def put(k, r0, value):
        hbuf[k, pl.ds(1 + r0, CHUNK)] = col_sum(value, masks)

    def window(k, r0):
        return hbuf[k, pl.ds(r0, CHUNK)] + hbuf[k, pl.ds(r0 + 1, CHUNK)] + hbuf[k, pl.ds(r0 + 2, CHUNK)]

    for r0 in range(0, 32, CHUNK):
        rows = pl.ds(r0, CHUNK)
        prod = srep[sg, 0, rows] * target_rows(tq, 0, tg, r0, CHUNK)
        prod += srep[sg, 1, rows] * target_rows(tq, 1, tg, r0, CHUNK)
        prod += srep[sg, 2, rows] * target_rows(tq, 2, tg, r0, CHUNK)
        put(0, r0, prod)
    total = None
    for layer in range(3):
        for r0 in range(0, 32, CHUNK):
            rows = pl.ds(r0, CHUNK)
            level = window(layer, r0) + BIAS_VAR
            x = level * gsrep[sg, layer, rows] * target_rows(gt, layer, tg, r0, CHUNK)
            rest = 1.0 - x * x
            root = lax.rsqrt(rest)
            xs[u, layer, rows] = x
            rs[u, layer, rows] = root
            value = x * horner(rest * root, NARROW if layer else WIDE, ALPHA if layer < 2 else BETA)
            if layer < 2:
                put(layer + 1, r0, value)
            else:
                part = jnp.sum(value, axis=0)
                total = part if total is None else total + part
    thacc[u] = total


def backward_unit(u, sg, tg, gsrep, gt, xs, rs, vs, us, hbuf, masks):
    for layer in (2, 1, 0):
        for r0 in range(0, 32, CHUNK):
            rows = pl.ds(r0, CHUNK)
            d = rs[u, layer, rows]
            if layer < 2:
                k = 2 - layer - 1
                d = d * (hbuf[k, pl.ds(r0, CHUNK)] + hbuf[k, pl.ds(r0 + 1, CHUNK)] + hbuf[k, pl.ds(r0 + 2, CHUNK)])
            vs[u, layer, rows] = d * xs[u, layer, rows]
            d = d * gsrep[sg, layer, rows] * target_rows(gt, layer, tg, r0, CHUNK)
            hbuf[2 - layer, pl.ds(1 + r0, CHUNK)] = col_sum(d, masks)
    for r0 in range(0, 32, CHUNK):
        us[u, pl.ds(r0, CHUNK)] = (
            hbuf[2, pl.ds(r0, CHUNK)] + hbuf[2, pl.ds(r0 + 1, CHUNK)] + hbuf[2, pl.ds(r0 + 2, CHUNK)]
        )


def fold_rows(r):
    lane = lanes((1, 128))
    low, even = lane < 64, (lane // 32) % 2 == 0
    y = [
        jnp.where(low, r[k], r[k + 2]) + roll_lanes(jnp.where(low, r[k + 2], r[k]), 64)
        for k in range(2)
    ]
    other = jnp.where(even, y[1], y[0])
    return jnp.where(even, y[0], y[1]) + jnp.where(even, roll_lanes(other, 96), roll_lanes(other, 32))


def contract_rows(sg, g, cot, tq, vs, us, nat):
    acc = [[None] * 4 for _ in range(6)]
    for tg in range(4):
        u = tg * 2 + sg
        weight = cot[u]
        for j in range(4):
            w = us[u, g * 4 + j] * weight
            terms = [w * tq[j, c, tg, pl.ds(g, 1), :] for c in range(3)]
            terms += [vs[u, layer, g * 4 + j] * weight for layer in range(3)]
            for q in range(6):
                acc[q][j] = terms[q] if tg == 0 else acc[q][j] + terms[q]
    for q in range(6):
        nat[sg, q, g] = fold_rows(acc[q])


def finish_supports(sg, nat, sbuf, slope_ref, gout, masks):
    def box(x):
        return box_natural(x[None], masks)[0]

    scale = (BETA * ALPHA * ALPHA, BETA * ALPHA, BETA)
    parts = [nat[sg, 3 + layer] * slope_ref[2 + layer, sg] * scale[layer] for layer in range(3)]
    d2 = parts[1] + box(parts[2]) * slope_ref[1, sg]
    d1 = parts[0] + box(d2) * slope_ref[0, sg]
    energy = box(d1) * (2.0 * PROD)
    for c in range(3):
        for g in range(8):
            at = pl.ds(sg * 8 * ROWS + c * 8 + g, 8, stride=ROWS)
            gout[at, :] = nat[sg, c, g] * (BETA * ALPHA * ALPHA * PROD) + energy[g] * sbuf[at, :]


def split_dot(x, ones):
    high = x.astype(bf16)
    rest = x - high.astype(f32)
    middle = rest.astype(bf16)
    low = (rest - middle.astype(f32)).astype(bf16)
    dot = lambda part: jnp.dot(part, ones, preferred_element_type=f32)
    return dot(high) + dot(middle) + dot(low)


def kernel(
    sup_in, coef_in, tgt_in, lab_in, out_ref, res_ref,
    sin, cin, tin, lin, sbuf, tbuf, meta, thall, gout, gbuf,
    srep, gsrep, slope_ref, tq, gt, xs, rs, hbuf, thacc, vs, us, cot, nat, expand, gather, spreadth,
    in_sem, ssend, tsend, csend, msend, thsend, gsend, srecv, trecv, krecv, crecv, mrecv, threcv, grecv,
):
    tgt, sup = lax.axis_index("tgt"), lax.axis_index("sup")
    z, xlo, core = sup // 4, (sup // 2) % 2, sup % 2
    a, b = xlo * 8 + tgt, z * 2 + core

    def plane(k):
        other = (a + k) % GROUP
        return (other % 8, z * 4 + (other // 8) * 2 + core), other

    def line(k):
        other = (b + k) % GROUP
        return (tgt, (other // 2) * 4 + xlo * 2 + other % 2)

    loads = [
        pltpu.make_async_copy(src, dst, in_sem.at[i])
        for i, (src, dst) in enumerate(((sup_in, sin), (coef_in, cin), (tgt_in, tin), (lab_in, lin)))
    ]
    for load in loads:
        load.start()
    barrier = pltpu.get_barrier_semaphore()
    for k in range(1, GROUP):
        pl.semaphore_signal(barrier, inc=1, device_id=plane(k)[0], device_id_type=MESH)
        pl.semaphore_signal(barrier, inc=1, device_id=line(k), device_id_type=MESH)

    hbuf[...] = jnp.zeros_like(hbuf)
    source = lax.broadcasted_iota(jnp.int32, (512, 128), 0) // 32
    gather[...] = (source == lanes((512, 128)) % 16).astype(f32).astype(bf16)
    source = lax.broadcasted_iota(jnp.int32, (128, 512), 0) % 16
    expand[...] = (source == lanes((128, 512)) // 32).astype(f32).astype(bf16)
    masks = col_masks()

    for load in loads:
        load.wait()
    own = pl.multiple_of(a * ROWS, 8)
    for g in range(8):
        for c in range(3):
            sbuf[pl.ds(own + c * 8 + g, 1), :] = sin[0, c : c + 1, g * 128 : g * 128 + 128]
            tbuf[b, pl.ds(c * 8 + g, 1), :] = tin[0, c : c + 1, g * 128 : g * 128 + 128]
    fill = jnp.zeros((8, 128 - LABELS), f32)
    meta[b, pl.ds(pl.multiple_of(xlo * 8, 8), 8), :] = jnp.concatenate([cin[...], fill], 1)
    meta[b, 16:17, :] = jnp.concatenate([lin[...], fill[:1]], 1)

    pl.semaphore_wait(barrier, 2 * (GROUP - 1))

    copies = []

    def send(src, dst, send_sem, recv_sem, device):
        copy = pltpu.make_async_remote_copy(
            src_ref=src, dst_ref=dst, send_sem=send_sem, recv_sem=recv_sem, device_id=device, device_id_type=MESH
        )
        copy.start()

    def all_arrived(ref, sem):
        pltpu.make_async_copy(ref, ref, sem).wait()

    sibling = (tgt, sup + 1 - 2 * core)
    order = (1, 7, 2, 6, 3, 5, 4)
    mine = tbuf.at[b]
    slab = sbuf.at[pl.ds(own, ROWS)]
    send(mine, mine, tsend, krecv, sibling)
    for i, d in enumerate(order):
        send(mine, mine, tsend, trecv.at[d], (tgt, ((z + d) % 8) * 4 + xlo * 2 + core))
        send(slab, slab, ssend, srecv, plane(2 * i + 1)[0])
        send(slab, slab, ssend, srecv, plane(2 * i + 2)[0])
    send(slab, slab, ssend, srecv, plane(15)[0])
    block = meta.at[b, pl.ds(pl.multiple_of(xlo * 8, 8), 8)]
    send(block, block, csend, crecv, (tgt, z * 4 + (1 - xlo) * 2 + core))
    for d in order:
        slot = tbuf.at[((z + 8 - d) % 8) * 2 + core]
        all_arrived(slot, trecv.at[d])
        send(slot, slot, tsend, krecv, sibling)
    others = sbuf.at[pl.ds(0, (GROUP - 1) * ROWS)]
    all_arrived(others, srecv)
    prepare_supports(sbuf, srep, gsrep, slope_ref, masks)
    all_arrived(block, crecv)
    for k in range(1, GROUP):
        send(meta.at[b], meta.at[b], msend, mrecv, line(k))
    all_arrived(tbuf.at[pl.ds(0, 8)], krecv)
    prepare_targets(tbuf, tq, gt, masks)

    @pl.loop(0, 8)
    def _(u):
        forward_unit(u, u % 2, u // 2, srep, gsrep, tq, gt, xs, rs, hbuf, thacc, masks)

    sums = jnp.concatenate(
        [jnp.concatenate([thacc[tg * 2 + sg] for tg in range(4)], 1) for sg in range(2)], 0
    )
    theta = split_dot(sums, gather[...]) + BIAS_VAR
    pick = (lax.broadcasted_iota(jnp.int32, (8, 128), 0) == lanes((8, 128)) // 16).astype(f32)
    for sg in range(2):
        thall[b, sg : sg + 1, :] = jnp.sum(theta[sg * 8 : sg * 8 + 8] * pick, axis=0, keepdims=True)
    for k in range(1, GROUP):
        send(thall.at[b], thall.at[b], thsend, threcv, line(k))

    @pl.loop(0, 8)
    def _(u):
        backward_unit(u, u % 2, u // 2, gsrep, gt, xs, rs, vs, us, hbuf, masks)

    all_arrived(meta.at[pl.ds(0, GROUP - 1)], mrecv)
    coeffs = meta[b, 0:16, :]
    coeffs_all = jnp.concatenate([meta[k, 0:16, :] for k in range(GROUP)], 0)
    labels = jnp.concatenate([meta[k, 16:17, :] for k in range(GROUP)], 0)
    contract_last = (((1,), (1,)), ((), ()))
    gram = lax.dot_general(coeffs, coeffs_all, contract_last, precision=HIGHEST, preferred_element_type=f32)
    wanted = lax.dot_general(coeffs, labels, contract_last, precision=HIGHEST, preferred_element_type=f32)
    wanted = jnp.concatenate([wanted, jnp.zeros((16, 112), f32)], 1)

    all_arrived(thall.at[pl.ds(0, GROUP - 1)], threcv)
    for k in range(GROUP):
        for sg in range(2):
            spreadth[pl.ds(k * 16 + sg * 8, 8), :] = thall[k, sg : sg + 1, :] * pick
    values = jnp.dot(gram, spreadth[...], precision=HIGHEST, preferred_element_type=f32) - wanted
    weights = split_dot(values, expand[...])
    for sg in range(2):
        for tg in range(4):
            cot[tg * 2 + sg] = weights[sg * 8 : sg * 8 + 8, tg * 128 : tg * 128 + 128]

    for sg in range(2):

        @pl.loop(0, 8)
        def _(g):
            contract_rows(sg, g, cot, tq, vs, us, nat)

        finish_supports(sg, nat, sbuf, slope_ref, gout, masks)
        for k in range(8):
            to = sg * 8 + (tgt + k) % 8
            if k == 0:

                @pl.when(sg != xlo)
                def _():
                    piece = gout.at[pl.ds(pl.multiple_of(to * ROWS, 8), ROWS)]
                    send(piece, gbuf.at[a], gsend, grecv, (tgt, z * 4 + sg * 2 + core))
            else:
                piece = gout.at[pl.ds(pl.multiple_of(to * ROWS, 8), ROWS)]
                send(piece, gbuf.at[a], gsend, grecv, ((tgt + k) % 8, z * 4 + sg * 2 + core))

    column = (lanes((1, 128)) % 16 == b).astype(f32)
    picked = jnp.sum(spreadth[...] * column, axis=1, keepdims=True)
    predicted = jnp.sum(picked * coeffs_all, axis=0, keepdims=True)
    res_ref[...] = (predicted - meta[b, 16:17, :])[:, :LABELS]

    gbuf[a] = gout[pl.ds(own, ROWS), :]
    all_arrived(gbuf.at[pl.ds(0, GROUP - 1)], grecv)
    total = gbuf[0]
    for k in range(1, GROUP):
        total = total + gbuf[k]
    out_ref[...] = total

    all_arrived(others, ssend)
    all_arrived(tbuf.at[pl.ds(0, GROUP - 1)], tsend)
    all_arrived(block, csend)
    all_arrived(meta.at[pl.ds(0, GROUP - 1)], msend)
    all_arrived(thall.at[pl.ds(0, GROUP - 1)], thsend)
    all_arrived(gbuf.at[pl.ds(0, GROUP - 1)], gsend)


def local(support, coeffs, targets, labels):
    vmem = lambda *shape: pltpu.VMEM(shape, f32)
    dma = pltpu.SemaphoreType.DMA
    grad, residual = pl.pallas_call(
        kernel,
        out_shape=(jax.ShapeDtypeStruct((ROWS, 128), f32), jax.ShapeDtypeStruct((1, LABELS), f32)),
        in_specs=[pl.BlockSpec(memory_space=pl.ANY)] * 4,
        out_specs=(pl.BlockSpec(memory_space=pltpu.VMEM), pl.BlockSpec(memory_space=pltpu.VMEM)),
        scratch_shapes=[
            vmem(1, 3, 1024), vmem(8, LABELS), vmem(1, 3, 1024), vmem(1, LABELS),
            vmem(GROUP * ROWS, 128), vmem(GROUP, ROWS, 128), vmem(GROUP, 17, 128), vmem(GROUP, 2, 128),
            vmem(GROUP * ROWS, 128), vmem(GROUP, ROWS, 128),
            vmem(2, 3, 32, 8, 128), vmem(2, 3, 32, 8, 128), vmem(5, 2, 8, 8, 128),
            vmem(4, 3, 4, 8, 128), vmem(4, 3, 4, 8, 128),
            vmem(8, 3, 32, 8, 128), vmem(8, 3, 32, 8, 128), vmem(3, 34, 8, 128), vmem(8, 8, 128),
            vmem(8, 3, 32, 8, 128), vmem(8, 32, 8, 128), vmem(8, 8, 128), vmem(2, 6, 8, 8, 128),
            pltpu.VMEM((128, 512), bf16), pltpu.VMEM((512, 128), bf16), vmem(256, 128),
            dma((4,)), dma, dma, dma, dma, dma, dma, dma, dma((8,)), dma, dma, dma, dma, dma,
        ],
        compiler_params=pltpu.CompilerParams(
            collective_id=0, has_side_effects=True, vmem_limit_bytes=48 * 1024 * 1024
        ),
    )(support, coeffs, targets, labels)
    return grad.reshape(1, 3, 1024), residual


def solution(mesh):
    return jax.shard_map(
        local,
        mesh=mesh,
        in_specs=(
            P(("sup", "tgt"), None, None),
            P("sup", None),
            P(("tgt", "sup"), None, None),
            P(("tgt", "sup"), None),
        ),
        out_specs=(P(("sup", "tgt"), None, None), P(("tgt", "sup"), None)),
        check_vma=False,
    )
```

time: 556 us -> 39 us (0.07); the launches traced: 546 us -> 38.7 us
  blocking collectives: 208 us -> 0 us
  local copies, waits for them, and re-layouts: 108 us -> 2.5 us
  waiting for transfers between devices: 84 us -> 0 us
  other arithmetic: 71.5 us -> 0 us
  matrix products: 59.7 us -> 0 us
  Pallas kernels: 0 us -> 35.6 us
  between operations: 14.7 us -> 0.67 us
    all_gather x3 -> x0, blocking collectives: 105 us -> none  [the longest x1 35.5 us: local(): lax.all_gather(targets, 'sup', axis=0, tiled=True)]
    psum x1 -> x0, blocking collectives: 104 us -> none  [local(): predicted = lax.psum(product(theta.T, coeffs), 'sup')]
    unnamed x2 -> x0, waiting for transfers between devices: 84 us -> none
    mul x20 -> x0, local copies, waits for them, and re-layouts: 66.1 us -> none  [the longest x18 58.1 us: pair_kernel(): 2.0 * kernel_level.reshape(SIDE, SIDE, sup_count, tgt_count)]
    dot_general x4 -> x0, matrix products: 59.7 us -> none  [the longest x2 59.3 us: pair_kernel(): jnp.einsum('scp,tcp->pst', support, targets, precision=lax.Precision.HIGH...]
    pallas_call x0 -> x1, Pallas kernels: none -> 35.6 us  [local(): pl.pallas_call(kernel, out_shape=(jax.ShapeDtypeStruct((ROWS, 128), f32),...]
    mul x9 -> x0, other arithmetic: 26.2 us -> none  [the longest x2 12.6 us: pair_kernel(): activated = 2.0 / math.pi * jnp.arcsin(correlation)]
    reduce_sum x6 -> x0, other arithmetic: 19.5 us -> none  [the longest x3 16.5 us: pair_kernel(): 2.0 * kernel_level.reshape(SIDE, SIDE, sup_count, tgt_count)]
  transfers between devices with their start and end apart: 1 -> 0, of which waited for: 1 -> 0; matrix products, arithmetic and copies ran while one was open for 0% -> 0% of each run, Pallas kernels for 0% -> 0%
where the time goes in v1:
time: 39 us; the launch traced here: 38.7 us
  Pallas kernels  35.6 us (91%)
  local copies, waits for them, and re-layouts  2.5 us (6%)
  between operations  0.67 us (2%)
    pallas_call x1, Pallas kernels, local(): pl.pallas_call(kernel, out_shape=(jax.ShapeDtypeStruct((ROWS, 128), f32),...  35.6 us
    unnamed x10, local copies, waits for them, and re-layouts  2.5 us

profile of v1, /device:TPU:2, one launch (start us, length us, event | category | flops | bytes accessed | tf_op | source)
XLA Modules:
  0.0 38.7 jit_solution(1103645935881832052)
XLA Ops:
  0.6 0.0 copy-start.2
  0.6 0.7 %copy.9.sup_in = f32[1,3,1024]{2,1,0:T(4,128)S(1)} copy(f32[1,3,1024]{2,0,1:T(1,128)} %param.4) | data formatting | bytes 24576 | tf_op args[0]
  1.4 0.0 copy-done.2
  1.4 0.0 copy-start
  1.4 0.0 copy-start.1
  1.4 0.7 %copy-done = f32[8,100]{1,0:T(8,128)S(1)} copy-done((f32[8,100]{1,0:T(8,128)S(1)}, f32[8,100]{1,0:T(8,128)}, u32[]{:S(2)}) %copy-start) | copy-done | bytes 3224
  2.0 0.0 copy-done.1
  2.1 35.6 %shard_map.59 = (f32[24,128]{1,0:T(8,128)S(1)}, f32[1,100]{1,0:T(1,128)S(1)}) custom-call(f32[1,3,1024]{2,1,0:T(4,128)S(1)} %copy.9.sup_in, f32[8,100]{1,0:T(8,128)S(1)} %copy-done, f32[1,3,1024]{2,1,0:T(4,128)S(1)} %copy.10.tgt_in, f32[1,100]{1,0:T(1,128)S(1)} %copy-done.1), custom_call_target="tpu_custom_call" | custom-call | tf_op jit(solution)/shard_map/pallas_call | solution.py:416
  37.6 0.6 %copy.14 = f32[1,3,1024]{2,0,1:T(1,128)} copy(f32[1,3,1024]{2,0,1:T(1,128)S(1)} %bitcast.1) | data formatting | bytes 24576
  38.2 0.5 %copy.15 = f32[1,100]{1,0:T(1,128)} copy(f32[1,100]{1,0:T(1,128)S(1)} %get-tuple-element.13) | data formatting | bytes 800
  (1 shorter events, 0.0 us)
Async XLA Ops:
  0.6 0.7 %copy-start.2 = (f32[1,3,1024]{2,0,1:T(1,128)S(1)}, f32[1,3,1024]{2,0,1:T(1,128)}, u32[]{:S(2)}) copy-start(f32[1,3,1024]{2,0,1:T(1,128)} %param.6) | copy-start | bytes 36868
  1.4 0.7 %copy-start = (f32[8,100]{1,0:T(8,128)S(1)}, f32[8,100]{1,0:T(8,128)}, u32[]{:S(2)}) copy-start(f32[8,100]{1,0:T(8,128)} %coef_in.1) | copy-start | bytes 9604
  1.4 0.7 %copy-start.1 = (f32[1,100]{1,0:T(1,128)S(1)}, f32[1,100]{1,0:T(1,128)}, u32[]{:S(2)}) copy-start(f32[1,100]{1,0:T(1,128)} %lab_in.1) | copy-start | bytes 1204

commit v2 on v1

--- a/solution.py
+++ b/solution.py
@@ -111,11 +111,12 @@
                     dst[sg, q % 3, g * 4 + j] = reps[j][g]
 
 
-def prepare_targets(tbuf, tq, gt, masks):
+def prepare_targets(half, slots, tbuf, tq, gt, masks):
     lane = lanes((1, 128))
     low, even = lane < 64, (lane // 32) % 2 == 0
-    for tg in range(4):
-        a = [tbuf[4 * tg + i] for i in range(4)]
+    for unit in range(2):
+        tg = 2 * half + unit
+        a = [tbuf[slots[tg][i]] for i in range(4)]
         p = [None] * 4
         for i in range(2):
             p[i] = jnp.where(low, a[i], pltpu.roll(a[i + 2], 64, 1))
@@ -126,28 +127,29 @@
             for c in range(3):
                 tq[2 * k, c, tg] = b0[c * 8 : c * 8 + 8]
                 tq[2 * k + 1, c, tg] = b1[c * 8 : c * 8 + 8]
-    x = [[tq[j, c].reshape(32, 128) for j in range(4)] for c in range(3)]
+    x = [[tq[j, c, 2 * half : 2 * half + 2].reshape(16, 128) for j in range(4)] for c in range(3)]
     energy = [(x[0][j] * x[0][j] + x[1][j] * x[1][j] + x[2][j] * x[2][j]) * PROD for j in range(4)]
-    g = lax.broadcasted_iota(jnp.int32, (32, 128), 0) % 8
+    g = lax.broadcasted_iota(jnp.int32, (16, 128), 0) % 8
     not_first, not_last = (g != 0).astype(f32), (g != 7).astype(f32)
 
     def box(values):
-        h = [col_sum(values[j * 32 : j * 32 + 32], masks) for j in range(4)]
+        flat = col_sum(values, masks)
+        h = [flat[j * 16 : j * 16 + 16] for j in range(4)]
         above = [pltpu.roll(h[3], 1, 0) * not_first] + h[:3]
-        below = h[1:] + [pltpu.roll(h[0], 31, 0) * not_last]
+        below = h[1:] + [pltpu.roll(h[0], 15, 0) * not_last]
         return jnp.concatenate([h[j] + above[j] + below[j] for j in range(4)], 0)
 
     gains, _ = self_chain(jnp.concatenate(energy, 0), box)
     for layer in range(3):
         for j in range(4):
-            gt[j, layer] = gains[layer][j * 32 : j * 32 + 32].reshape(4, 8, 128)
+            gt[j, layer, 2 * half : 2 * half + 2] = gains[layer][j * 16 : j * 16 + 16].reshape(2, 8, 128)
 
 
 def target_rows(ref, q, tg, first, count):
     return jnp.concatenate([ref[r % 4, q, tg, pl.ds(r // 4, 1), :][None] for r in range(first, first + count)], 0)
 
 
-CHUNK = 8
+CHUNK = 16
 
 
 def forward_unit(u, sg, tg, srep, gsrep, tq, gt, xs, rs, hbuf, thacc, masks):
@@ -199,30 +201,32 @@
         )
 
 
-def fold_rows(r):
-    lane = lanes((1, 128))
-    low, even = lane < 64, (lane // 32) % 2 == 0
-    y = [
-        jnp.where(low, r[k], r[k + 2]) + roll_lanes(jnp.where(low, r[k + 2], r[k]), 64)
-        for k in range(2)
-    ]
-    other = jnp.where(even, y[1], y[0])
-    return jnp.where(even, y[0], y[1]) + jnp.where(even, roll_lanes(other, 96), roll_lanes(other, 32))
-
-
-def contract_rows(sg, g, cot, tq, vs, us, nat):
-    acc = [[None] * 4 for _ in range(6)]
-    for tg in range(4):
-        u = tg * 2 + sg
-        weight = cot[u]
+def fold_rows(rows):
+    block = lanes((1, 1, 128)) // 32
+    r = (rows[1], rows[2], rows[3], rows[0])
+    low, middle, odd = block < 2, (block == 1) | (block == 2), block % 2 == 1
+    y0 = jnp.where(low, r[0], r[2]) + roll_lanes(jnp.where(low, r[2], r[0]), 64)
+    y1 = jnp.where(middle, r[1], r[3]) + roll_lanes(jnp.where(middle, r[3], r[1]), 64)
+    return jnp.where(odd, y0, y1) + roll_lanes(jnp.where(odd, y1, y0), 32)
+
+
+def contract_rows(sg, cot, tq, vs, us, accs, nat):
+    @pl.loop(0, 8)
+    def _(g):
         for j in range(4):
-            w = us[u, g * 4 + j] * weight
-            terms = [w * tq[j, c, tg, pl.ds(g, 1), :] for c in range(3)]
-            terms += [vs[u, layer, g * 4 + j] * weight for layer in range(3)]
+            acc = [None] * 6
+            for tg in range(4):
+                u = tg * 2 + sg
+                weight = cot[u]
+                w = us[u, g * 4 + j] * weight
+                terms = [w * tq[j, c, tg, pl.ds(g, 1), :] for c in range(3)]
+                terms += [vs[u, layer, g * 4 + j] * weight for layer in range(3)]
+                acc = [term if tg == 0 else old + term for old, term in zip(acc, terms)]
             for q in range(6):
-                acc[q][j] = terms[q] if tg == 0 else acc[q][j] + terms[q]
+                accs[q, j, g] = acc[q]
+
     for q in range(6):
-        nat[sg, q, g] = fold_rows(acc[q])
+        nat[sg, q] = fold_rows([accs[q, j] for j in range(4)])
 
 
 def finish_supports(sg, nat, sbuf, slope_ref, gout, masks):
@@ -251,8 +255,8 @@
 
 def kernel(
     sup_in, coef_in, tgt_in, lab_in, out_ref, res_ref,
-    sin, cin, tin, lin, sbuf, tbuf, meta, thall, gout, gbuf,
-    srep, gsrep, slope_ref, tq, gt, xs, rs, hbuf, thacc, vs, us, cot, nat, expand, gather, spreadth,
+    cin, lin, sbuf, tbuf, meta, thall, gout, gbuf,
+    srep, gsrep, slope_ref, tq, gt, xs, rs, hbuf, thacc, vs, us, cot, accs, nat, expand, gather, spreadth,
     in_sem, ssend, tsend, csend, msend, thsend, gsend, srecv, trecv, krecv, crecv, mrecv, threcv, grecv,
 ):
     tgt, sup = lax.axis_index("tgt"), lax.axis_index("sup")
@@ -267,38 +271,40 @@
         other = (b + k) % GROUP
         return (tgt, (other // 2) * 4 + xlo * 2 + other % 2)
 
-    loads = [
-        pltpu.make_async_copy(src, dst, in_sem.at[i])
-        for i, (src, dst) in enumerate(((sup_in, sin), (coef_in, cin), (tgt_in, tin), (lab_in, lin)))
-    ]
-    for load in loads:
-        load.start()
     barrier = pltpu.get_barrier_semaphore()
     for k in range(1, GROUP):
         pl.semaphore_signal(barrier, inc=1, device_id=plane(k)[0], device_id_type=MESH)
         pl.semaphore_signal(barrier, inc=1, device_id=line(k), device_id_type=MESH)
+    own = pl.multiple_of(a * ROWS, 8)
+    mine = tbuf.at[b]
+    slab = sbuf.at[pl.ds(own, ROWS)]
+    loads = [
+        pltpu.make_async_copy(src, dst, in_sem.at[i])
+        for i, (src, dst) in enumerate(((sup_in, slab), (tgt_in, mine), (coef_in, cin), (lab_in, lin)))
+    ]
+    for load in loads:
+        load.start()
 
     hbuf[...] = jnp.zeros_like(hbuf)
-    source = lax.broadcasted_iota(jnp.int32, (512, 128), 0) // 32
-    gather[...] = (source == lanes((512, 128)) % 16).astype(f32).astype(bf16)
-    source = lax.broadcasted_iota(jnp.int32, (128, 512), 0) % 16
-    expand[...] = (source == lanes((128, 512)) // 32).astype(f32).astype(bf16)
+    slots = [[((z + step + 8) % 8) * 2 + i for step in (-k, k + 1) for i in range(2)] for k in range(4)]
+
+    def slot_of(place):
+        unit, i = place // 4, place % 4
+        return ((jnp.where(i < 2, -unit, unit + 1) + z + 8) % 8) * 2 + i % 2
+
+    place = lax.broadcasted_iota(jnp.int32, (512, 128), 0) // 32
+    gather[...] = (slot_of(place) == lanes((512, 128)) % 16).astype(f32).astype(bf16)
+    place = lanes((128, 512)) // 32
+    expand[...] = (slot_of(place) == lax.broadcasted_iota(jnp.int32, (128, 512), 0) % 16).astype(f32).astype(bf16)
     masks = col_masks()
 
     for load in loads:
         load.wait()
-    own = pl.multiple_of(a * ROWS, 8)
-    for g in range(8):
-        for c in range(3):
-            sbuf[pl.ds(own + c * 8 + g, 1), :] = sin[0, c : c + 1, g * 128 : g * 128 + 128]
-            tbuf[b, pl.ds(c * 8 + g, 1), :] = tin[0, c : c + 1, g * 128 : g * 128 + 128]
     fill = jnp.zeros((8, 128 - LABELS), f32)
     meta[b, pl.ds(pl.multiple_of(xlo * 8, 8), 8), :] = jnp.concatenate([cin[...], fill], 1)
     meta[b, 16:17, :] = jnp.concatenate([lin[...], fill[:1]], 1)
 
     pl.semaphore_wait(barrier, 2 * (GROUP - 1))
-
-    copies = []
 
     def send(src, dst, send_sem, recv_sem, device):
         copy = pltpu.make_async_remote_copy(
@@ -310,10 +316,8 @@
         pltpu.make_async_copy(ref, ref, sem).wait()
 
     sibling = (tgt, sup + 1 - 2 * core)
-    order = (1, 7, 2, 6, 3, 5, 4)
-    mine = tbuf.at[b]
-    slab = sbuf.at[pl.ds(own, ROWS)]
-    send(mine, mine, tsend, krecv, sibling)
+    order = (7, 1, 6, 2, 5, 3, 4)
+    send(mine, mine, tsend, krecv.at[0], sibling)
     for i, d in enumerate(order):
         send(mine, mine, tsend, trecv.at[d], (tgt, ((z + d) % 8) * 4 + xlo * 2 + core))
         send(slab, slab, ssend, srecv, plane(2 * i + 1)[0])
@@ -321,22 +325,33 @@
     send(slab, slab, ssend, srecv, plane(15)[0])
     block = meta.at[b, pl.ds(pl.multiple_of(xlo * 8, 8), 8)]
     send(block, block, csend, crecv, (tgt, z * 4 + (1 - xlo) * 2 + core))
-    for d in order:
-        slot = tbuf.at[((z + 8 - d) % 8) * 2 + core]
-        all_arrived(slot, trecv.at[d])
-        send(slot, slot, tsend, krecv, sibling)
+
+    def pass_on(steps, half):
+        for d in steps:
+            slot = tbuf.at[((z + 8 - d) % 8) * 2 + core]
+            all_arrived(slot, trecv.at[d])
+            send(slot, slot, tsend, krecv.at[half], sibling)
+
+    def forward_half(half):
+        @pl.loop(0, 4)
+        def _(i):
+            sg, tg = i % 2, 2 * half + i // 2
+            forward_unit(tg * 2 + sg, sg, tg, srep, gsrep, tq, gt, xs, rs, hbuf, thacc, masks)
+
+    pass_on(order[:3], 0)
+    all_arrived(tbuf.at[pl.ds(0, 4)], krecv.at[0])
+    prepare_targets(0, slots, tbuf, tq, gt, masks)
+    pass_on(order[3:], 1)
     others = sbuf.at[pl.ds(0, (GROUP - 1) * ROWS)]
     all_arrived(others, srecv)
-    prepare_supports(sbuf, srep, gsrep, slope_ref, masks)
     all_arrived(block, crecv)
     for k in range(1, GROUP):
         send(meta.at[b], meta.at[b], msend, mrecv, line(k))
-    all_arrived(tbuf.at[pl.ds(0, 8)], krecv)
-    prepare_targets(tbuf, tq, gt, masks)
-
-    @pl.loop(0, 8)
-    def _(u):
-        forward_unit(u, u % 2, u // 2, srep, gsrep, tq, gt, xs, rs, hbuf, thacc, masks)
+    prepare_supports(sbuf, srep, gsrep, slope_ref, masks)
+    forward_half(0)
+    all_arrived(tbuf.at[pl.ds(0, 4)], krecv.at[1])
+    prepare_targets(1, slots, tbuf, tq, gt, masks)
+    forward_half(1)
 
     sums = jnp.concatenate(
         [jnp.concatenate([thacc[tg * 2 + sg] for tg in range(4)], 1) for sg in range(2)], 0
@@ -372,11 +387,7 @@
             cot[tg * 2 + sg] = weights[sg * 8 : sg * 8 + 8, tg * 128 : tg * 128 + 128]
 
     for sg in range(2):
-
-        @pl.loop(0, 8)
-        def _(g):
-            contract_rows(sg, g, cot, tq, vs, us, nat)
-
+        contract_rows(sg, cot, tq, vs, us, accs, nat)
         finish_supports(sg, nat, sbuf, slope_ref, gout, masks)
         for k in range(8):
             to = sg * 8 + (tgt + k) % 8
@@ -410,29 +421,48 @@
     all_arrived(gbuf.at[pl.ds(0, GROUP - 1)], gsend)
 
 
+def write(grad_in, res_in, grad_out, res_out, sem):
+    copies = [
+        pltpu.make_async_copy(src, dst, sem.at[i])
+        for i, (src, dst) in enumerate(((grad_in, grad_out), (res_in, res_out)))
+    ]
+    for copy in copies:
+        copy.start()
+    for copy in copies:
+        copy.wait()
+
+
 def local(support, coeffs, targets, labels):
     vmem = lambda *shape: pltpu.VMEM(shape, f32)
     dma = pltpu.SemaphoreType.DMA
     grad, residual = pl.pallas_call(
         kernel,
-        out_shape=(jax.ShapeDtypeStruct((ROWS, 128), f32), jax.ShapeDtypeStruct((1, LABELS), f32)),
-        in_specs=[pl.BlockSpec(memory_space=pl.ANY)] * 4,
+        out_shape=(pltpu.VMEM((ROWS, 128), f32), pltpu.VMEM((1, LABELS), f32)),
+        in_specs=[pl.BlockSpec(memory_space=pltpu.HBM)] * 4,
         out_specs=(pl.BlockSpec(memory_space=pltpu.VMEM), pl.BlockSpec(memory_space=pltpu.VMEM)),
         scratch_shapes=[
-            vmem(1, 3, 1024), vmem(8, LABELS), vmem(1, 3, 1024), vmem(1, LABELS),
+            vmem(8, LABELS), vmem(1, LABELS),
             vmem(GROUP * ROWS, 128), vmem(GROUP, ROWS, 128), vmem(GROUP, 17, 128), vmem(GROUP, 2, 128),
             vmem(GROUP * ROWS, 128), vmem(GROUP, ROWS, 128),
             vmem(2, 3, 32, 8, 128), vmem(2, 3, 32, 8, 128), vmem(5, 2, 8, 8, 128),
             vmem(4, 3, 4, 8, 128), vmem(4, 3, 4, 8, 128),
             vmem(8, 3, 32, 8, 128), vmem(8, 3, 32, 8, 128), vmem(3, 34, 8, 128), vmem(8, 8, 128),
-            vmem(8, 3, 32, 8, 128), vmem(8, 32, 8, 128), vmem(8, 8, 128), vmem(2, 6, 8, 8, 128),
+            vmem(8, 3, 32, 8, 128), vmem(8, 32, 8, 128), vmem(8, 8, 128), vmem(6, 4, 8, 8, 128), vmem(2, 6, 8, 8, 128),
             pltpu.VMEM((128, 512), bf16), pltpu.VMEM((512, 128), bf16), vmem(256, 128),
-            dma((4,)), dma, dma, dma, dma, dma, dma, dma, dma((8,)), dma, dma, dma, dma, dma,
+            dma((4,)), dma, dma, dma, dma, dma, dma, dma, dma((8,)), dma((2,)), dma, dma, dma, dma,
         ],
         compiler_params=pltpu.CompilerParams(
-            collective_id=0, has_side_effects=True, vmem_limit_bytes=48 * 1024 * 1024
+            collective_id=0, has_side_effects=True, vmem_limit_bytes=56000 * 1024
         ),
-    )(support, coeffs, targets, labels)
+    )(support.reshape(ROWS, 128), coeffs, targets.reshape(ROWS, 128), labels)
+    grad, residual = pl.pallas_call(
+        write,
+        out_shape=(jax.ShapeDtypeStruct((ROWS, 128), f32), jax.ShapeDtypeStruct((1, LABELS), f32)),
+        in_specs=[pl.BlockSpec(memory_space=pltpu.VMEM)] * 2,
+        out_specs=(pl.BlockSpec(memory_space=pltpu.HBM), pl.BlockSpec(memory_space=pltpu.HBM)),
+        scratch_shapes=[dma((2,))],
+        compiler_params=pltpu.CompilerParams(vmem_limit_bytes=1024 * 1024),
+    )(grad, residual)
     return grad.reshape(1, 3, 1024), residual
 
 

time: 39 us -> 34.7 us (0.89)
  local copies, waits for them, and re-layouts: 2.5 us -> 0 us
  Pallas kernels: 35.6 us -> 33.9 us
    unnamed x10 -> x0, local copies, waits for them, and re-layouts: 2.5 us -> none
    pallas_call x1 -> x2, Pallas kernels: 35.6 us -> 33.9 us  [the longest x1 33.3 us: local(): pl.pallas_call(kernel, out_shape=(pltpu.VMEM((ROWS, 128), f32), pltpu.VME...]
where the time goes in v2:
time: 34.7 us; the launch traced here: 34.5 us
  Pallas kernels  33.9 us (98%)
  between operations  0.64 us (2%)
    pallas_call x1, Pallas kernels, local(): pl.pallas_call(kernel, out_shape=(pltpu.VMEM((ROWS, 128), f32), pltpu.VME...  33.3 us

profile of v2, /device:TPU:2, one launch (start us, length us, event | category | flops | bytes accessed | tf_op | source)
XLA Modules:
  0.0 34.5 jit_solution(3036507085078114520)
XLA Ops:
  0.6 33.3 %shard_map.59 = (f32[24,128]{1,0:T(8,128)S(1)}, f32[1,100]{1,0:T(1,128)S(1)}) custom-call(f32[24,128]{1,0:T(8,128)} %bitcast.3, f32[8,100]{1,0:T(8,128)} %coef_in.1, f32[24,128]{1,0:T(8,128)} %bitcast.4, f32[1,100]{1,0:T(1,128)} %lab_in.1), custom_call_target="tpu_custom_call" | custom-call | tf_op jit(solution)/shard_map/pallas_call | solution.py:438
  33.9 0.6 %shard_map.60 = (f32[24,128]{1,0:T(8,128)}, f32[1,100]{1,0:T(1,128)}) custom-call(f32[24,128]{1,0:T(8,128)S(1)} %get-tuple-element.6.grad_in, f32[1,100]{1,0:T(1,128)S(1)} %get-tuple-element.7.res_in), custom_call_target="tpu_custom_call" | custom-call | tf_op jit(solution)/shard_map/pallas_call | solution.py:458

commit v3 on v2

v3 whole, which is shorter than its diff:
```python
import math

import jax
import jax.numpy as jnp
from jax import lax
from jax.experimental import pallas as pl
from jax.experimental.pallas import tpu as pltpu
from jax.sharding import PartitionSpec as P

f32 = jnp.float32
bf16 = jnp.bfloat16
MESH = pl.DeviceIdType.MESH
HIGHEST = lax.Precision.HIGHEST

WEIGHT_VAR = 1.6
BIAS_VAR = 0.1
LABELS = 100

GROUP = 16
ROWS = 24
SPREAD = WEIGHT_VAR / 9.0
PROD = SPREAD / 3.0
ALPHA = SPREAD * 2.0 / math.pi
BETA = WEIGHT_VAR / 1024.0 * 2.0 / math.pi

WIDE = (
    1.5707956460959935, -0.999909759045268, 0.7833927466035577, -0.6491778438734823, 0.5105887741390924,
    -0.3261364828462018, 0.1375277539431936, -0.027081268358035065,
)
NARROW = (1.5592713649848087, -0.9171235094499794, 0.5296910993035006, -0.21179670068297385, 0.039958000056267685)

PLANE = sorted(
    ((dx, dy) for dx in range(4) for dy in range(4) if dx or dy), key=lambda p: -min(p[0], 4 - p[0]) - min(p[1], 4 - p[1])
)
LINE = sorted(((dz, dc) for dz in range(8) for dc in range(2) if dz or dc), key=lambda p: -min(p[0], 8 - p[0]))
FAR_Z = (4, 5, 3, 6, 2, 7, 1)


def horner(w, coefs, scale):
    total = jnp.full_like(w, coefs[-1] * scale)
    for coef in coefs[-2::-1]:
        total = total * w + coef * scale
    return total


def lanes(shape):
    return lax.broadcasted_iota(jnp.int32, shape, len(shape) - 1)


def roll_lanes(x, shift):
    flat = x.reshape(-1, 128)
    return pltpu.roll(flat, shift, 1).reshape(x.shape)


def col_sum(x, masks):
    return x + roll_lanes(x, 1) * masks[0] + roll_lanes(x, 127) * masks[1]


def col_masks():
    col = lanes((1, 128)) % 32
    return (col != 0).astype(f32), (col != 31).astype(f32)


def self_chain(energy, box):
    gains, slopes = [], []
    level = box(energy) + BIAS_VAR
    for layer in range(3):
        gain = lax.rsqrt(1.0 + 2.0 * level)
        gains.append(gain)
        if layer < 2:
            square = gain * gain
            root = lax.rsqrt(1.0 + 4.0 * level)
            w = (1.0 + 4.0 * level) * root * square
            value = 2.0 * level * square * horner(w, NARROW if layer else WIDE, ALPHA)
            slopes.append((4.0 / math.pi * SPREAD) * square * root)
            level = box(value) + BIAS_VAR
    return gains, slopes


def box_natural(x, masks):
    h = col_sum(x, masks)
    lane = lanes((1, 1, 1, 128))
    zero = jnp.zeros_like(h[:, :1])
    above = roll_lanes(h, 32)
    below = roll_lanes(h, 96)
    above = jnp.where(lane < 32, jnp.concatenate([zero, above[:, :-1]], 1), above)
    below = jnp.where(lane >= 96, jnp.concatenate([below[:, 1:], zero], 1), below)
    return h + above + below


def prepare_supports(sbuf, srep, gsrep, slope_ref, masks):
    chans = [
        jnp.stack([sbuf[pl.ds(sg * 8 * ROWS + c * 8 + g, 8, stride=ROWS), :] for sg in range(2) for g in range(8)])
        for c in range(3)
    ]
    energy = (chans[0] * chans[0] + chans[1] * chans[1] + chans[2] * chans[2]) * PROD
    gains, slopes = self_chain(energy.reshape(2, 8, 8, 128), lambda x: box_natural(x, masks))
    for layer in range(2):
        slope_ref[layer] = slopes[layer]
    for layer in range(3):
        slope_ref[2 + layer] = -(gains[layer] * gains[layer])
    lane = lanes((1, 128))
    low, even = lane < 64, (lane // 32) % 2 == 0
    for q in range(6):
        src = chans[q] * PROD if q < 3 else gains[q - 3].reshape(16, 8, 128) * 2.0
        dst = srep if q < 3 else gsrep
        turned = roll_lanes(src, 64)
        first, second = jnp.where(low, src, turned), jnp.where(low, turned, src)
        t1, t2 = roll_lanes(first, 32), roll_lanes(second, 32)
        reps = (jnp.where(even, first, t1), jnp.where(even, t1, first), jnp.where(even, second, t2), jnp.where(even, t2, second))
        for j in range(4):
            for sg in range(2):
                for g in range(8):
                    dst[sg, q % 3, g * 4 + j] = reps[j][sg * 8 + g]


def prepare_targets(half, slots, tbuf, tq, gt, masks):
    lane = lanes((1, 128))
    low, even = lane < 64, (lane // 32) % 2 == 0
    for unit in range(2):
        tg = 2 * half + unit
        a = [tbuf[slots[tg][i]] for i in range(4)]
        p = [None] * 4
        for i in range(2):
            p[i] = jnp.where(low, a[i], pltpu.roll(a[i + 2], 64, 1))
            p[i + 2] = jnp.where(low, pltpu.roll(a[i], 64, 1), a[i + 2])
        for k in range(2):
            b0 = jnp.where(even, p[2 * k], pltpu.roll(p[2 * k + 1], 32, 1))
            b1 = jnp.where(even, pltpu.roll(p[2 * k], 96, 1), p[2 * k + 1])
            for c in range(3):
                tq[2 * k, c, tg] = b0[c * 8 : c * 8 + 8]
                tq[2 * k + 1, c, tg] = b1[c * 8 : c * 8 + 8]
    x = [[tq[j, c, 2 * half : 2 * half + 2].reshape(16, 128) for j in range(4)] for c in range(3)]
    energy = [(x[0][j] * x[0][j] + x[1][j] * x[1][j] + x[2][j] * x[2][j]) * PROD for j in range(4)]
    g = lax.broadcasted_iota(jnp.int32, (16, 128), 0) % 8
    not_first, not_last = (g != 0).astype(f32), (g != 7).astype(f32)

    def box(values):
        flat = col_sum(values, masks)
        h = [flat[j * 16 : j * 16 + 16] for j in range(4)]
        above = [pltpu.roll(h[3], 1, 0) * not_first] + h[:3]
        below = h[1:] + [pltpu.roll(h[0], 15, 0) * not_last]
        return jnp.concatenate([h[j] + above[j] + below[j] for j in range(4)], 0)

    gains, _ = self_chain(jnp.concatenate(energy, 0), box)
    for layer in range(3):
        for j in range(4):
            gt[j, layer, 2 * half : 2 * half + 2] = gains[layer][j * 16 : j * 16 + 16].reshape(2, 8, 128)


def target_rows(ref, q, tg, first, count):
    return jnp.concatenate([ref[r % 4, q, tg, pl.ds(r // 4, 1), :][None] for r in range(first, first + count)], 0)


CHUNK = 8


def forward_unit(tg, srep, gsrep, tq, gt, xs, rs, hbuf, thacc, masks):
    def put(k, r0, value):
        hbuf[k, :, pl.ds(1 + r0, CHUNK)] = col_sum(value, masks)

    for r0 in range(0, 32, CHUNK):
        rows = pl.ds(r0, CHUNK)
        prod = srep[:, 0, rows] * target_rows(tq, 0, tg, r0, CHUNK)[None]
        prod += srep[:, 1, rows] * target_rows(tq, 1, tg, r0, CHUNK)[None]
        prod += srep[:, 2, rows] * target_rows(tq, 2, tg, r0, CHUNK)[None]
        put(0, r0, prod)
    total = None
    for layer in range(3):
        for r0 in range(0, 32, CHUNK):
            rows = pl.ds(r0, CHUNK)
            level = row_sum(hbuf, layer, r0) + BIAS_VAR
            x = level * gsrep[:, layer, rows] * target_rows(gt, layer, tg, r0, CHUNK)[None]
            rest = 1.0 - x * x
            root = lax.rsqrt(rest)
            xs[tg, :, layer, rows] = x
            rs[tg, :, layer, rows] = root
            value = x * horner(rest * root, NARROW if layer else WIDE, ALPHA if layer < 2 else BETA)
            if layer < 2:
                put(layer + 1, r0, value)
            else:
                part = jnp.sum(value, axis=1)
                total = part if total is None else total + part
    thacc[tg] = total


def row_sum(hbuf, k, r0):
    row = [hbuf[k, :, pl.ds(r0 + i, 1)] for i in range(CHUNK + 2)]
    sums = []
    for i in range(1, CHUNK + 1, 2):
        both = row[i] + row[i + 1]
        sums += [row[i - 1] + both, both + row[i + 2]]
    return jnp.concatenate(sums, 1)


def backward_unit(tg, gsrep, gt, xs, rs, vs, us, hbuf, masks):
    for layer in (2, 1, 0):
        for r0 in range(0, 32, CHUNK):
            rows = pl.ds(r0, CHUNK)
            d = rs[tg, :, layer, rows]
            if layer < 2:
                d = d * row_sum(hbuf, 1 - layer, r0)
            vs[tg, :, layer, rows] = d * xs[tg, :, layer, rows]
            d = d * gsrep[:, layer, rows] * target_rows(gt, layer, tg, r0, CHUNK)[None]
            hbuf[2 - layer, :, pl.ds(1 + r0, CHUNK)] = col_sum(d, masks)
    for r0 in range(0, 32, CHUNK):
        us[tg, :, pl.ds(r0, CHUNK)] = row_sum(hbuf, 2, r0)


def fold_rows(rows):
    block = lanes((1, 1, 128)) // 32
    r = (rows[1], rows[2], rows[3], rows[0])
    low, middle, odd = block < 2, (block == 1) | (block == 2), block % 2 == 1
    y0 = jnp.where(low, r[0], r[2]) + roll_lanes(jnp.where(low, r[2], r[0]), 64)
    y1 = jnp.where(middle, r[1], r[3]) + roll_lanes(jnp.where(middle, r[3], r[1]), 64)
    return jnp.where(odd, y0, y1) + roll_lanes(jnp.where(odd, y1, y0), 32)


def contract_rows(sg, cot, tq, vs, us, accs, nat):
    @pl.loop(0, 8, unroll=True)
    def _(g):
        for j in range(4):
            acc = [None] * 6
            for tg in range(4):
                weight = cot[tg]
                w = us[tg, sg, g * 4 + j] * weight
                terms = [w * tq[j, c, tg, pl.ds(g, 1), :] for c in range(3)]
                terms += [vs[tg, sg, layer, g * 4 + j] * weight for layer in range(3)]
                acc = [term if tg == 0 else old + term for old, term in zip(acc, terms)]
            for q in range(6):
                accs[q, j, g] = acc[q]

    for q in range(6):
        nat[sg, q] = fold_rows([accs[q, j] for j in range(4)])


def finish_supports(sg, nat, sbuf, slope_ref, gout, masks):
    def box(x):
        return box_natural(x[None], masks)[0]

    scale = (BETA * ALPHA * ALPHA, BETA * ALPHA, BETA)
    parts = [nat[sg, 3 + layer] * slope_ref[2 + layer, sg] * scale[layer] for layer in range(3)]
    d2 = parts[1] + box(parts[2]) * slope_ref[1, sg]
    d1 = parts[0] + box(d2) * slope_ref[0, sg]
    energy = box(d1) * (2.0 * PROD)
    for c in range(3):
        for g in range(8):
            at = pl.ds(sg * (8 * ROWS) + c * 8 + g, 8, stride=ROWS)
            gout[at, :] = nat[sg, c, g] * (BETA * ALPHA * ALPHA * PROD) + energy[g] * sbuf[at, :]


def split_dot(x, ones):
    high = x.astype(bf16)
    rest = x - high.astype(f32)
    middle = rest.astype(bf16)
    low = (rest - middle.astype(f32)).astype(bf16)
    dot = lambda part: jnp.dot(part, ones, preferred_element_type=f32)
    return dot(high) + dot(middle) + dot(low)


def kernel(
    sup_in, coef_in, tgt_in, lab_in, out_ref, res_ref,
    cin, lin, sbuf, tbuf, meta, meta2, thall, gout, gbuf,
    srep, gsrep, slope_ref, tq, gt, xs, rs, hbuf, thacc, vs, us, cot, accs, nat, expand, gather, spreadth,
    in_sem, ssend, tsend, csend, msend, thsend, gsend, srecv, trecv, krecv, crecv, mrecv, threcv, grecv,
):
    tgt, sup = lax.axis_index("tgt"), lax.axis_index("sup")
    z, xlo, core = sup // 4, (sup // 2) % 2, sup % 2
    a, b = xlo * 8 + tgt, z * 2 + core

    y, x = tgt // 2, (tgt % 2) * 2 + xlo

    def plane(dx, dy):
        to = (x + dx) % 4
        return (((y + dy) % 4) * 2 + to // 2, z * 4 + (to % 2) * 2 + core)

    def line(dz, dc):
        return (tgt, ((z + dz) % 8) * 4 + xlo * 2 + (core + dc) % 2)

    barrier = pltpu.get_barrier_semaphore()
    for near, far in zip(PLANE, LINE):
        pl.semaphore_signal(barrier, inc=1, device_id=plane(*near), device_id_type=MESH)
        pl.semaphore_signal(barrier, inc=1, device_id=line(*far), device_id_type=MESH)
    own = pl.multiple_of(a * ROWS, 8)
    mine = tbuf.at[b]
    slab = sbuf.at[pl.ds(own, ROWS)]
    loads = [
        pltpu.make_async_copy(src, dst, in_sem.at[i])
        for i, (src, dst) in enumerate(((sup_in, slab), (tgt_in, mine), (coef_in, cin), (lab_in, lin)))
    ]
    for load in loads:
        load.start()

    masks = col_masks()

    for load in loads:
        load.wait()
    fill = jnp.zeros((8, 128 - LABELS), f32)
    meta[b, 0:8, :] = jnp.concatenate([cin[...], fill], 1)
    meta[b, 8:9, :] = jnp.concatenate([lin[...], fill[:1]], 1)

    pl.semaphore_wait(barrier, 2 * (GROUP - 1))

    def send(src, dst, send_sem, recv_sem, device):
        copy = pltpu.make_async_remote_copy(
            src_ref=src, dst_ref=dst, send_sem=send_sem, recv_sem=recv_sem, device_id=device, device_id_type=MESH
        )
        copy.start()

    def all_arrived(ref, sem):
        pltpu.make_async_copy(ref, ref, sem).wait()

    sibling = (tgt, sup + 1 - 2 * core)
    order = (7, 1, 6, 2, 5, 3, 4)
    for i, d in enumerate(FAR_Z):
        send(mine, mine, tsend, trecv.at[d], line(d, 0))
        send(slab, slab, ssend, srecv, plane(*PLANE[2 * i]))
        send(slab, slab, ssend, srecv, plane(*PLANE[2 * i + 1]))
    send(slab, slab, ssend, srecv, plane(*PLANE[14]))
    send(mine, mine, tsend, krecv.at[0], sibling)

    def pass_on(steps, half):
        for d in steps:
            slot = tbuf.at[((z + 8 - d) % 8) * 2 + core]
            all_arrived(slot, trecv.at[d])
            send(slot, slot, tsend, krecv.at[half], sibling)

    def forward_half(half):
        @pl.loop(0, 2)
        def _(i):
            forward_unit(2 * half + i, srep, gsrep, tq, gt, xs, rs, hbuf, thacc, masks)

    hbuf[...] = jnp.zeros_like(hbuf)
    slots = [[((z + step + 8) % 8) * 2 + i for step in (-k, k + 1) for i in range(2)] for k in range(4)]

    def slot_of(place):
        unit, i = place // 4, place % 4
        return ((jnp.where(i < 2, -unit, unit + 1) + z + 8) % 8) * 2 + i % 2

    place = lax.broadcasted_iota(jnp.int32, (512, 128), 0) // 32
    gather[...] = (slot_of(place) == lanes((512, 128)) % 16).astype(f32).astype(bf16)
    place = lanes((128, 512)) // 32
    expand[...] = (slot_of(place) == lax.broadcasted_iota(jnp.int32, (128, 512), 0) % 16).astype(f32).astype(bf16)
    pass_on(order[:3], 0)
    all_arrived(tbuf.at[pl.ds(0, 4)], krecv.at[0])
    prepare_targets(0, slots, tbuf, tq, gt, masks)
    pass_on(order[3:], 1)
    others = sbuf.at[pl.ds(0, (GROUP - 1) * ROWS)]
    all_arrived(others, srecv)
    prepare_supports(sbuf, srep, gsrep, slope_ref, masks)
    for step in LINE:
        send(meta.at[b], meta.at[b], msend, mrecv, line(*step))
    forward_half(0)
    all_arrived(tbuf.at[pl.ds(0, 4)], krecv.at[1])
    prepare_targets(1, slots, tbuf, tq, gt, masks)
    forward_half(1)

    sums = jnp.concatenate(
        [jnp.concatenate([thacc[tg, sg] for tg in range(4)], 1) for sg in range(2)], 0
    )
    theta = split_dot(sums, gather[...]) + BIAS_VAR
    pick = (lax.broadcasted_iota(jnp.int32, (8, 128), 0) == lanes((8, 128)) // 16).astype(f32)
    for sg in range(2):
        thall[b, sg : sg + 1, :] = jnp.sum(theta[sg * 8 : sg * 8 + 8] * pick, axis=0, keepdims=True)
    for step in LINE:
        send(thall.at[b], thall.at[b], thsend, threcv, line(*step))

    all_arrived(meta.at[pl.ds(0, GROUP - 1)], mrecv)
    send(meta, meta2, csend, crecv, (tgt, z * 4 + (1 - xlo) * 2 + core))
    @pl.loop(0, 4)
    def _(tg):
        backward_unit(tg, gsrep, gt, xs, rs, vs, us, hbuf, masks)

    all_arrived(meta2, crecv)
    coeffs = jnp.concatenate([meta[b, 0:8, :], meta2[b, 0:8, :]], 0)
    coeffs_all = jnp.concatenate([ref[k, 0:8, :] for ref in (meta, meta2) for k in range(GROUP)], 0)
    labels = jnp.concatenate([meta[k, 8:9, :] for k in range(GROUP)], 0)
    contract_last = (((1,), (1,)), ((), ()))
    gram = lax.dot_general(coeffs, coeffs_all, contract_last, precision=HIGHEST, preferred_element_type=f32)
    wanted = lax.dot_general(coeffs, labels, contract_last, precision=HIGHEST, preferred_element_type=f32)
    wanted = jnp.concatenate([wanted, jnp.zeros((16, 112), f32)], 1)

    all_arrived(thall.at[pl.ds(0, GROUP - 1)], threcv)
    for other in range(2):
        for k in range(GROUP):
            spreadth[pl.ds(other * 128 + k * 8, 8), :] = thall[k, pl.ds((xlo + other) % 2, 1), :] * pick
    values = jnp.dot(gram, spreadth[...], precision=HIGHEST, preferred_element_type=f32) - wanted
    weights = split_dot(values, expand[...])
    for other in range(2):
        for tg in range(4):
            cot[tg, other] = weights[other * 8 : other * 8 + 8, tg * 128 : tg * 128 + 128]

    for other in range(2):
        sg = (xlo + other) % 2
        contract_rows(sg, cot[:, other], tq, vs, us, accs, nat)
        finish_supports(sg, nat, sbuf, slope_ref, gout, masks)
        for dx, dy in PLANE:
            if dx % 2 == other:
                to_tgt, to_sup = plane(dx, dy)
                piece = gout.at[pl.ds(pl.multiple_of((sg * 8 + to_tgt) * ROWS, 8), ROWS)]
                send(piece, gbuf.at[a], gsend, grecv, (to_tgt, to_sup))

    column = (lanes((1, 128)) % 16 == b).astype(f32)
    picked = jnp.sum(spreadth[...] * column, axis=1, keepdims=True)
    predicted = jnp.sum(picked * coeffs_all, axis=0, keepdims=True)
    res_ref[...] = (predicted - meta[b, 8:9, :])[:, :LABELS]

    gbuf[a] = gout[pl.ds(own, ROWS), :]
    all_arrived(gbuf.at[pl.ds(0, GROUP - 1)], grecv)
    total = gbuf[0]
    for k in range(1, GROUP):
        total = total + gbuf[k]
    out_ref[...] = total

    all_arrived(others, ssend)
    all_arrived(tbuf.at[pl.ds(0, GROUP - 1)], tsend)
    all_arrived(meta2, csend)
    all_arrived(meta.at[pl.ds(0, GROUP - 1)], msend)
    all_arrived(thall.at[pl.ds(0, GROUP - 1)], thsend)
    all_arrived(gbuf.at[pl.ds(0, GROUP - 1)], gsend)


def write(grad_in, res_in, grad_out, res_out, sem):
    copies = [
        pltpu.make_async_copy(src, dst, sem.at[i])
        for i, (src, dst) in enumerate(((grad_in, grad_out), (res_in, res_out)))
    ]
    for copy in copies:
        copy.start()
    for copy in copies:
        copy.wait()


def local(support, coeffs, targets, labels):
    vmem = lambda *shape: pltpu.VMEM(shape, f32)
    dma = pltpu.SemaphoreType.DMA
    grad, residual = pl.pallas_call(
        kernel,
        out_shape=(pltpu.VMEM((ROWS, 128), f32), pltpu.VMEM((1, LABELS), f32)),
        in_specs=[pl.BlockSpec(memory_space=pltpu.HBM)] * 4,
        out_specs=(pl.BlockSpec(memory_space=pltpu.VMEM), pl.BlockSpec(memory_space=pltpu.VMEM)),
        scratch_shapes=[
            vmem(8, LABELS), vmem(1, LABELS),
            vmem(GROUP * ROWS, 128), vmem(GROUP, ROWS, 128), vmem(GROUP, 9, 128), vmem(GROUP, 9, 128), vmem(GROUP, 2, 128),
            vmem(GROUP * ROWS, 128), vmem(GROUP, ROWS, 128),
            vmem(2, 3, 32, 8, 128), vmem(2, 3, 32, 8, 128), vmem(5, 2, 8, 8, 128),
            vmem(4, 3, 4, 8, 128), vmem(4, 3, 4, 8, 128),
            vmem(4, 2, 3, 32, 8, 128), vmem(4, 2, 3, 32, 8, 128), vmem(3, 2, 34, 8, 128), vmem(4, 2, 8, 128),
            vmem(4, 2, 3, 32, 8, 128), vmem(4, 2, 32, 8, 128), vmem(4, 2, 8, 128), vmem(6, 4, 8, 8, 128), vmem(2, 6, 8, 8, 128),
            pltpu.VMEM((128, 512), bf16), pltpu.VMEM((512, 128), bf16), vmem(256, 128),
            dma((4,)), dma, dma, dma, dma, dma, dma, dma, dma((8,)), dma((2,)), dma, dma, dma, dma,
        ],
        compiler_params=pltpu.CompilerParams(
            collective_id=0, has_side_effects=True, vmem_limit_bytes=56000 * 1024
        ),
    )(support.reshape(ROWS, 128), coeffs, targets.reshape(ROWS, 128), labels)
    grad, residual = pl.pallas_call(
        write,
        out_shape=(jax.ShapeDtypeStruct((ROWS, 128), f32), jax.ShapeDtypeStruct((1, LABELS), f32)),
        in_specs=[pl.BlockSpec(memory_space=pltpu.VMEM)] * 2,
        out_specs=(pl.BlockSpec(memory_space=pltpu.HBM), pl.BlockSpec(memory_space=pltpu.HBM)),
        scratch_shapes=[dma((2,))],
        compiler_params=pltpu.CompilerParams(vmem_limit_bytes=1024 * 1024),
    )(grad, residual)
    return grad.reshape(1, 3, 1024), residual


def solution(mesh):
    return jax.shard_map(
        local,
        mesh=mesh,
        in_specs=(
            P(("sup", "tgt"), None, None),
            P("sup", None),
            P(("tgt", "sup"), None, None),
            P(("tgt", "sup"), None),
        ),
        out_specs=(P(("sup", "tgt"), None, None), P(("tgt", "sup"), None)),
        check_vma=False,
    )
```

time: 34.7 us -> 33.2 us (0.957)
  the two profiles are of different devices: /device:TPU:2 before, /device:TPU:1 now
where the time goes in v3:
time: 33.2 us; the launch traced here: 33.1 us
  Pallas kernels  32.4 us (98%)
  between operations  0.64 us (2%)
    pallas_call x1, Pallas kernels, local(): pl.pallas_call(kernel, out_shape=(pltpu.VMEM((ROWS, 128), f32), pltpu.VME...  31.8 us

profile of v3, /device:TPU:1, one launch (start us, length us, event | category | flops | bytes accessed | tf_op | source)
XLA Modules:
  0.0 33.1 jit_solution(10081992153121338268)
XLA Ops:
  0.6 31.8 %shard_map.59 = (f32[24,128]{1,0:T(8,128)S(1)}, f32[1,100]{1,0:T(1,128)S(1)}) custom-call(f32[24,128]{1,0:T(8,128)} %bitcast.3, f32[8,100]{1,0:T(8,128)} %coef_in.1, f32[24,128]{1,0:T(8,128)} %bitcast.4, f32[1,100]{1,0:T(1,128)} %lab_in.1), custom_call_target="tpu_custom_call" | custom-call | tf_op jit(solution)/shard_map/pallas_call | solution.py:437
  32.4 0.6 %shard_map.60 = (f32[24,128]{1,0:T(8,128)}, f32[1,100]{1,0:T(1,128)}) custom-call(f32[24,128]{1,0:T(8,128)S(1)} %get-tuple-element.6.grad_in, f32[1,100]{1,0:T(1,128)S(1)} %get-tuple-element.7.res_in), custom_call_target="tpu_custom_call" | custom-call | tf_op jit(solution)/shard_map/pallas_call | solution.py:457

commit v4 on v3

--- a/solution.py
+++ b/solution.py
@@ -326,7 +326,7 @@
             send(slot, slot, tsend, krecv.at[half], sibling)
 
     def forward_half(half):
-        @pl.loop(0, 2)
+        @pl.loop(0, 2, unroll=True)
         def _(i):
             forward_unit(2 * half + i, srep, gsrep, tq, gt, xs, rs, hbuf, thacc, masks)
 
@@ -367,7 +367,7 @@
 
     all_arrived(meta.at[pl.ds(0, GROUP - 1)], mrecv)
     send(meta, meta2, csend, crecv, (tgt, z * 4 + (1 - xlo) * 2 + core))
-    @pl.loop(0, 4)
+    @pl.loop(0, 4, unroll=True)
     def _(tg):
         backward_unit(tg, gsrep, gt, xs, rs, vs, us, hbuf, masks)
 

time: 33.2 us -> 32.6 us (0.982)
  Pallas kernels: 32.4 us -> 31.8 us
    pallas_call x1, Pallas kernels: 31.8 us -> 31.2 us  [local(): pl.pallas_call(kernel, out_shape=(pltpu.VMEM((ROWS, 128), f32), pltpu.VME...]
where the time goes in v4:
time: 32.6 us; the launch traced here: 32.5 us
  Pallas kernels  31.8 us (98%)
  between operations  0.64 us (2%)
    pallas_call x1, Pallas kernels, local(): pl.pallas_call(kernel, out_shape=(pltpu.VMEM((ROWS, 128), f32), pltpu.VME...  31.2 us

profile of v4, /device:TPU:1, one launch (start us, length us, event | category | flops | bytes accessed | tf_op | source)
XLA Modules:
  0.0 32.5 jit_solution(15656331332108536444)
XLA Ops:
  0.6 31.2 %shard_map.59 = (f32[24,128]{1,0:T(8,128)S(1)}, f32[1,100]{1,0:T(1,128)S(1)}) custom-call(f32[24,128]{1,0:T(8,128)} %bitcast.3, f32[8,100]{1,0:T(8,128)} %coef_in.1, f32[24,128]{1,0:T(8,128)} %bitcast.4, f32[1,100]{1,0:T(1,128)} %lab_in.1), custom_call_target="tpu_custom_call" | custom-call | tf_op jit(solution)/shard_map/pallas_call | solution.py:437
  31.8 0.6 %shard_map.60 = (f32[24,128]{1,0:T(8,128)}, f32[1,100]{1,0:T(1,128)}) custom-call(f32[24,128]{1,0:T(8,128)S(1)} %get-tuple-element.6.grad_in, f32[1,100]{1,0:T(1,128)S(1)} %get-tuple-element.7.res_in), custom_call_target="tpu_custom_call" | custom-call | tf_op jit(solution)/shard_map/pallas_call | solution.py:457
